TPU v7x, 512 devices: a whole 4x4x16 slice. The times are simulated.
512 devices in a mesh: row: 32 (over x, y, core), col: 16 (over z).
Axes of the slice: x: 4, y: 4, z: 16, core: 2. Of those that a mesh axis runs over, the one named last changes fastest.
Arguments:
- diag_factor: float32 [1024, 1024], P('row', 'col'), may hold values from -1 to 2.5, as said below
- panel_factor: float32 [16384, 1024], P('row', 'col'), may hold values from -0.046875 to 0.046875
- left_factor: float32 [16384, 8192], P('row', 'col'), may hold values from -0.046875 to 0.046875
- pivot_factor: float32 [1024, 8192], P('row', 'col'), may hold values from -0.1875 to 0.1875
- panel_adjoint: float32 [16384, 1024], P('row', 'col'), may hold values from -6 to 6
- left_adjoint: float32 [16384, 8192], P('row', 'col'), may hold values from -6 to 6
- pivot_adjoint: float32 [1024, 8192], P('row', 'col'), may hold values from -6 to 6
- diag_adjoint: float32 [1024, 1024], P('row', 'col'), may hold values from -6 to 6
Outputs:
- solved_panel: float32 [16384, 1024], P('row', 'col')
- left_out: float32 [16384, 8192], P('row', 'col')
- pivot_out: float32 [1024, 8192], P('row', 'col')
- diag_out: float32 [1024, 1024], P('row', 'col')
Inputs may be any that keep to these rules, and one draw needn't show every extreme that they name: diag_factor is lower triangular: zero above the diagonal, diagonal entries at least 1.
All inputs are finite; a program needn't handle non-finite values.
Results may differ from a plain program's by a relative error of at most 0.000073.
Values sent between devices are 32-bit elements; how exact they have to be, the bound alone decides.
A program may use at most 64 MiB of HBM per device.

v0:
```python
import jax
import jax.numpy as jnp
from jax import lax
from jax.sharding import PartitionSpec as P


def right_solve(tile, source):
    return jax.scipy.linalg.solve_triangular(tile, source.T, trans="T", lower=True).T


def local(
    diag_factor,
    panel_factor,
    left_factor,
    pivot_factor,
    panel_adjoint,
    left_adjoint,
    pivot_adjoint,
    diag_adjoint,
):
    highest = lax.Precision.HIGHEST
    block_width = panel_adjoint.shape[1]
    my_col = lax.axis_index("col")
    my_row = lax.axis_index("row")
    column_block = lax.all_gather(diag_factor, "row", axis=0, tiled=True)
    whole_diag = lax.all_gather(column_block, "col", axis=1, tiled=True)
    full_rows = lax.all_gather(panel_adjoint, "col", axis=1, tiled=True)
    solved = right_solve(whole_diag, full_rows)
    solved_panel = lax.dynamic_slice_in_dim(solved, my_col * block_width, block_width, 1)
    picked = solved
    left_out = left_adjoint - jnp.dot(
        picked,
        lax.all_gather(pivot_factor, "row", axis=0, tiled=True),
        precision=highest,
        preferred_element_type=jnp.float32,
    )
    own_rows = diag_adjoint.shape[0]
    picked = solved
    pivot_sum = lax.psum_scatter(
        jnp.einsum("rk,rc->kc", picked, left_factor, precision=highest),
        "row",
        scatter_dimension=0,
        tiled=True,
    )
    picked = solved
    square_sum = lax.psum_scatter(
        jnp.einsum("rk,rc->kc", picked, panel_factor, precision=highest),
        "row",
        scatter_dimension=0,
        tiled=True,
    )
    pivot_out = pivot_adjoint - pivot_sum
    global_row = my_row * own_rows + lax.broadcasted_iota(jnp.int32, (own_rows, block_width), 0)
    global_col = my_col * block_width + lax.broadcasted_iota(jnp.int32, (own_rows, block_width), 1)
    diag_out = diag_adjoint - jnp.where(global_col <= global_row, square_sum, 0.0)
    return (solved_panel, left_out, pivot_out, diag_out)


def solution(mesh):
    in_specs = (
        P("row", "col"),
        P("row", "col"),
        P("row", "col"),
        P("row", "col"),
        P("row", "col"),
        P("row", "col"),
        P("row", "col"),
        P("row", "col"),
    )
    out_specs = (P("row", "col"), P("row", "col"), P("row", "col"), P("row", "col"))
    return jax.shard_map(local, mesh=mesh, in_specs=in_specs, out_specs=out_specs, check_vma=False)
```

profile of v0, /device:TPU:2, one launch (start us, length us, event | category | flops | bytes accessed | tf_op | source)
XLA Modules:
  0.0 463.6 jit_solution(8965409141635587499)
XLA Ops:
  7.2 27.8 %all_gather.12 = f32[1024,64]{1,0:T(8,128)S(1)} all-gather(f32[32,64]{1,0:T(8,128)} %param.8), channel_id=1, replica_groups=mesh['row'=32,'col'=16] {'row'}, dimensions={0}, use_global_device_ids=true | all-gather | bytes 270336 | tf_op jit(solution)/shard_map/all_gather | solution.py:25
  35.0 0.9 copy.14
  36.0 0.7 all-gather.6.cloned.1.call-update
  36.7 0.7 all-gather.8.cloned.1.call-update
  37.5 77.2 %all-gather.4.cloned.1.call-done = f32[1024,1024]{0,1:T(8,128)} async-done(((f32[1024,64]{0,1:T(8,128)}), f32[1024,1024]{0,1:T(8,128)}) %all-gather.4.cloned.1.call-update) | async-done | bytes 4194320 | tf_op jit(solution)/shard_map/all_gather | solution.py:26
  114.7 4.8 %fusion = f32[1024,1024]{0,1:T(8,128)} fusion(f32[1024,1024]{0,1:T(8,128)} %all-gather.4.cloned.1.call-done), kind=kLoop, calls=%fused_computation.3 | loop fusion | flops 2097152 | bytes 8388608 | tf_op jit(solution)/shard_map/jit(_solve_triangular)/triangular_solve | solution.py:8
  119.5 24.1 %while.1 = (s32[]{:T(128)}, f32[1024,1024]{0,1:T(8,128)}, s32[8,2]{0,1:T(2,128)S(1)}, f32[8,128,128]{2,1,0:T(8,128)S(1)}, s32[]{:T(128)}) while((s32[]{:T(128)}, f32[1024,1024]{0,1:T(8,128)}, s32[8,2]{0,1:T(2,128)S(1)}, f32[8,128,128]{2,1,0:T(8,128)S(1)}, s32[]{:T(128)}) %tuple.28), condition=%wide.while_cond, body=%wide.while_body.sunk | while | flops 2 | bytes 393321 | solution.py:8
  120.1 2.3 dynamic-slice.12
  123.1 2.3 dynamic-slice.12
  126.1 2.3 dynamic-slice.12
  129.1 2.3 dynamic-slice.12
  132.2 2.3 dynamic-slice.12
  135.2 2.3 dynamic-slice.12
  138.2 2.3 dynamic-slice.12
  141.2 2.2 dynamic-slice.12
  143.6 78.6 %custom-call.4 = f32[8,128,128]{1,2,0:T(8,128)S(1)} custom-call(f32[8,128,128]{2,1,0:T(8,128)S(1)} %get-tuple-element.11), custom_call_target="InvertDiagBlocksLowerTriangular" | custom-call | tf_op jit(solution)/shard_map/jit(_solve_triangular)/triangular_solve | solution.py:8
  222.2 1.5 fusion.19
  223.8 1.4 convolution_subtract_fusion.4
  225.5 1.4 convolution_subtract_fusion.3
  227.3 1.6 convolution_subtract_fusion.6
  229.3 1.7 convolution_subtract_fusion.7
  231.4 1.9 convolution_subtract_fusion.2
  233.8 2.0 convolution_subtract_fusion.5
  236.4 2.2 convolution_subtract_fusion.1
  238.6 1.2 convolution_dynamic-update-slice_fusion
  240.1 2.6 fusion.36
  243.0 4.8 %fusion.35 = f32[1024,512]{1,0:T(8,128)} fusion(f32[1024,512]{1,0:T(8,128)S(1)} %constant_dynamic-update-slice_fusion.18, f32[512,512]{1,0:T(8,128)S(1)} %copy-done), kind=kOutput, calls=%fused_computation.85 | convolution fusion | flops 3221225472 | bytes 5242880 | tf_op jit(solution)/shard_map/rk,rc->kc/dot_general | solution.py:40
  248.5 6.3 %convolution_subtract_fusion = f32[512,512]{1,0:T(8,128)} fusion(f32[512,512]{1,0:T(8,128)} %param.13, f32[1024,512]{1,0:T(8,128)S(1)} %constant_dynamic-update-slice_fusion.18, f32[1024,512]{1,0:T(8,128)} %all-gather.8.cloned.1.call-done), kind=kOutput, calls=%fused_computation.4 | convolution fusion | flops 3221487616 | bytes 6291456 | tf_op jit(solution)/shard_map/dot_general | solution.py:31
  254.9 95.1 %reduce-scatter.5.cloned.1.call-done = f32[32,64]{1,0:T(8,128)} async-done(((f32[1024,64]{1,0:T(8,128)}), f32[32,64]{1,0:T(8,128)}) %reduce-scatter.5.cloned.1.call-update) | async-done | bytes 8208 | tf_op jit(solution)/shard_map/reduce_scatter | solution.py:46
  349.9 1.4 select_subtract_fusion
  351.3 104.3 %reduce-scatter.3.cloned.1.call-done = f32[32,512]{1,0:T(8,128)} async-done(((f32[1024,512]{1,0:T(8,128)}), f32[32,512]{1,0:T(8,128)}) %reduce-scatter.3.cloned.1.call-update) | async-done | bytes 65552 | tf_op jit(solution)/shard_map/reduce_scatter | solution.py:39
  455.6 1.5 sub.10
  (88 shorter events, 9.4 us)
Async XLA Ops:
  7.2 235.8 %copy-start = (f32[512,512]{1,0:T(8,128)S(1)}, f32[512,512]{1,0:T(8,128)}, u32[]{:S(2)}) copy-start(f32[512,512]{1,0:T(8,128)} %param.10) | copy-start | bytes 3145732
  7.2 107.5 %all-gather.4.cloned.1.call-start = ((), (), s32[]{:S(2)}) async-start(), calls=%async_computation.2 | async-start | bytes 4456448 | tf_op jit(solution)/shard_map/all_gather | solution.py:26
  35.9 186.3 %all-gather.6.cloned.1.call-start = ((), (), s32[]{:S(2)}) async-start(), calls=%async_computation.3 | async-start | bytes 2228224 | tf_op jit(solution)/shard_map/all_gather | solution.py:27
  36.7 211.8 %all-gather.8.cloned.1.call-start = ((), (), s32[]{:S(2)}) async-start(), calls=%async_computation.4 | async-start | bytes 2162688 | tf_op jit(solution)/shard_map/all_gather | solution.py:33
  37.4 312.5 %reduce-scatter.5.cloned.1.call-start = ((), (), s32[]{:S(2)}) async-start(), calls=%async_computation.6 | async-start | bytes 540672 | tf_op jit(solution)/shard_map/reduce_scatter | solution.py:46
  222.2 13.7 %copy-start.2 = (f32[8,128,128]{1,2,0:T(8,128)}, f32[8,128,128]{1,2,0:T(8,128)S(1)}, u32[]{:S(2)}) copy-start(f32[8,128,128]{1,2,0:T(8,128)S(1)} %custom-call.4) | copy-start | bytes 1572868
  222.2 5.1 %copy-start.1 = (f32[512,1024]{0,1:T(8,128)S(1)}, f32[512,1024]{0,1:T(8,128)}, u32[]{:S(2)}) copy-start(f32[512,1024]{0,1:T(8,128)} %all-gather.6.cloned.1.call-done) | copy-start | bytes 6291460
  238.6 1.5 copy-start.3
  242.7 212.9 %reduce-scatter.3.cloned.1.call-start = ((), (), s32[]{:S(2)}) async-start(), calls=%async_computation.5 | async-start | bytes 2162688 | tf_op jit(solution)/shard_map/reduce_scatter | solution.py:39
  248.5 101.4 %copy-start.5 = (f32[32,64]{1,0:T(8,128)S(1)}, f32[32,64]{1,0:T(8,128)}, u32[]{:S(2)}) copy-start(f32[32,64]{1,0:T(8,128)} %param.15) | copy-start | bytes 24580
  248.5 207.1 %copy-start.4 = (f32[32,512]{1,0:T(8,128)S(1)}, f32[32,512]{1,0:T(8,128)}, u32[]{:S(2)}) copy-start(f32[32,512]{1,0:T(8,128)} %param.14) | copy-start | bytes 196612
Sparse Core Ops, SparseCore 0:
  36.0 78.6 all-gather.3
  116.8 70.5 all-gather.5
  190.5 55.6 all-gather.7
  250.3 99.5 reduce-scatter.4
  354.2 101.3 reduce-scatter.2
where the time goes:
time: 465 us; the launch traced here: 464 us
  waiting for transfers between devices  278 us (60%)
  other arithmetic  86.2 us (19%)
  matrix products  30.8 us (7%)
  blocking collectives  27.8 us (6%)
  local copies, waits for them, and re-layouts  25.9 us (6%)
  between operations  14.2 us (3%)
    reduce_scatter x1, waiting for transfers between devices, local(): lax.psum_scatter(jnp.einsum('rk,rc->kc', picked, left_factor, precision=h...  104 us
    reduce_scatter x1, waiting for transfers between devices, local(): lax.psum_scatter(jnp.einsum('rk,rc->kc', picked, panel_factor, precision=...  95.1 us
    another operation x3, other arithmetic, right_solve(): jax.scipy.linalg.solve_triangular(tile, source.T, trans='T', lower=True)  83.4 us
    all_gather x1, waiting for transfers between devices, local(): whole_diag = lax.all_gather(column_block, 'col', axis=1, tiled=True)  77.2 us
    all_gather x1, blocking collectives, local(): column_block = lax.all_gather(diag_factor, 'row', axis=0, tiled=True)  27.8 us
    another operation x40, local copies, waits for them, and re-layouts  23.8 us
    another operation x15, matrix products, right_solve(): jax.scipy.linalg.solve_triangular(tile, source.T, trans='T', lower=True)  17.1 us
  transfers between devices with their start and end apart: 5, of which 3 were waited for; matrix products, arithmetic and copies ran while one was open for 30% of the time, Pallas kernels for 0%

commit v1 on v0

--- a/solution.py
+++ b/solution.py
@@ -23,8 +23,13 @@
     my_col = lax.axis_index("col")
     my_row = lax.axis_index("row")
     column_block = lax.all_gather(diag_factor, "row", axis=0, tiled=True)
-    whole_diag = lax.all_gather(column_block, "col", axis=1, tiled=True)
-    full_rows = lax.all_gather(panel_adjoint, "col", axis=1, tiled=True)
+    whole_diag, full_rows = jnp.split(
+        lax.all_gather(
+            jnp.concatenate([column_block, panel_adjoint], axis=0), "col", axis=1, tiled=True
+        ),
+        [column_block.shape[0]],
+        axis=0,
+    )
     solved = right_solve(whole_diag, full_rows)
     solved_panel = lax.dynamic_slice_in_dim(solved, my_col * block_width, block_width, 1)
     picked = solved

time: 465 us -> 463 us (level)
    reduce_scatter x1, waiting for transfers between devices: 95.1 us -> 84.4 us  [local(): lax.psum_scatter(jnp.einsum('rk,rc->kc', picked, panel_factor, precision=...]
    all_gather x2 -> x1, waiting for transfers between devices: 77.3 us -> 85.3 us  [local(): lax.all_gather(jnp.concatenate([column_block, panel_adjoint], axis=0), 'c...]
  transfers between devices with their start and end apart: 5 -> 4, of which waited for: 3 -> 3; matrix products, arithmetic and copies ran while one was open for 30% -> 31% of each run, Pallas kernels for 0% -> 0%
where the time goes in v1:
time: 463 us; the launch traced here: 462 us
  waiting for transfers between devices  275 us (59%)
  other arithmetic  86.3 us (19%)
  matrix products  29.4 us (6%)
  local copies, waits for them, and re-layouts  29 us (6%)
  blocking collectives  27.6 us (6%)
  between operations  14.2 us (3%)
    reduce_scatter x1, waiting for transfers between devices, local(): lax.psum_scatter(jnp.einsum('rk,rc->kc', picked, left_factor, precision=h...  104 us
    all_gather x1, waiting for transfers between devices, local(): lax.all_gather(jnp.concatenate([column_block, panel_adjoint], axis=0), 'c...  85.3 us
    reduce_scatter x1, waiting for transfers between devices, local(): lax.psum_scatter(jnp.einsum('rk,rc->kc', picked, panel_factor, precision=...  84.4 us
    another operation x3, other arithmetic, right_solve(): jax.scipy.linalg.solve_triangular(tile, source.T, trans='T', lower=True)  83.4 us
    all_gather x1, blocking collectives, local(): column_block = lax.all_gather(diag_factor, 'row', axis=0, tiled=True)  27.6 us
    another operation x40, local copies, waits for them, and re-layouts  23.8 us
    another operation x15, matrix products, right_solve(): jax.scipy.linalg.solve_triangular(tile, source.T, trans='T', lower=True)  15.7 us
  transfers between devices with their start and end apart: 4, of which 3 were waited for; matrix products, arithmetic and copies ran while one was open for 31% of the time, Pallas kernels for 0%

profile of v1, /device:TPU:2, one launch (start us, length us, event | category | flops | bytes accessed | tf_op | source)
XLA Modules:
  0.0 462.0 jit_solution(16928641645007432970)
XLA Ops:
  7.2 1.1 copy.15
  8.3 27.6 %all_gather.9 = f32[1024,64]{1,0:T(8,128)S(1)} all-gather(f32[32,64]{1,0:T(8,128)} %param.8), channel_id=1, replica_groups=mesh['row'=32,'col'=16] {'row'}, dimensions={0}, use_global_device_ids=true | all-gather | bytes 270336 | tf_op jit(solution)/shard_map/all_gather | solution.py:25
  36.0 1.0 copy.16
  37.1 0.7 all-gather.5.cloned.1.call-update
  37.9 85.3 %all-gather.3.cloned.1.call-done = f32[1536,1024]{0,1:T(8,128)} async-done(((f32[1536,64]{0,1:T(8,128)}), f32[1536,1024]{0,1:T(8,128)}) %all-gather.3.cloned.1.call-update) | async-done | bytes 6291472 | tf_op jit(solution)/shard_map/all_gather | solution.py:27
  123.2 4.8 %slice_select_fusion = f32[1024,1024]{0,1:T(8,128)} fusion(f32[1536,1024]{0,1:T(8,128)} %all-gather.3.cloned.1.call-done), kind=kLoop, calls=%fused_computation.2 | loop fusion | flops 2097152 | bytes 8388608 | tf_op jit(solution)/shard_map/jit(_solve_triangular)/triangular_solve | solution.py:8
  128.0 24.1 %while.1 = (s32[]{:T(128)}, f32[1024,1024]{0,1:T(8,128)}, s32[8,2]{0,1:T(2,128)S(1)}, f32[8,128,128]{2,1,0:T(8,128)S(1)}, s32[]{:T(128)}) while((s32[]{:T(128)}, f32[1024,1024]{0,1:T(8,128)}, s32[8,2]{0,1:T(2,128)S(1)}, f32[8,128,128]{2,1,0:T(8,128)S(1)}, s32[]{:T(128)}) %tuple.28), condition=%wide.while_cond, body=%wide.while_body.sunk | while | flops 2 | bytes 393329 | solution.py:8
  128.6 2.3 dynamic-slice.12
  131.6 2.3 dynamic-slice.12
  134.7 2.3 dynamic-slice.12
  137.7 2.3 dynamic-slice.12
  140.7 2.3 dynamic-slice.12
  143.7 2.3 dynamic-slice.12
  146.8 2.3 dynamic-slice.12
  149.8 2.2 dynamic-slice.12
  152.1 78.6 %custom-call.4 = f32[8,128,128]{1,2,0:T(8,128)S(1)} custom-call(f32[8,128,128]{2,1,0:T(8,128)S(1)} %get-tuple-element.11), custom_call_target="InvertDiagBlocksLowerTriangular" | custom-call | tf_op jit(solution)/shard_map/jit(_solve_triangular)/triangular_solve | solution.py:8
  230.8 2.0 slice_bitcast_fusion
  233.1 1.2 convolution_subtract_fusion.4
  234.7 1.3 convolution_subtract_fusion.3
  236.4 1.6 convolution_subtract_fusion.6
  238.3 1.7 convolution_subtract_fusion.7
  240.5 1.9 convolution_subtract_fusion.2
  242.9 2.0 convolution_subtract_fusion.5
  245.4 2.2 convolution_subtract_fusion.1
  247.7 1.2 convolution_dynamic-update-slice_fusion
  249.1 2.6 fusion.35
  252.1 4.8 %fusion.34 = f32[1024,512]{1,0:T(8,128)} fusion(f32[1024,512]{1,0:T(8,128)S(1)} %constant_dynamic-update-slice_fusion.18, f32[512,512]{1,0:T(8,128)S(1)} %copy-done), kind=kOutput, calls=%fused_computation.87 | convolution fusion | flops 3221225472 | bytes 5242880 | tf_op jit(solution)/shard_map/rk,rc->kc/dot_general | solution.py:45
  257.6 6.4 %convolution_subtract_fusion = f32[512,512]{1,0:T(8,128)} fusion(f32[512,512]{1,0:T(8,128)} %param.13, f32[1024,512]{1,0:T(8,128)S(1)} %constant_dynamic-update-slice_fusion.18, f32[1024,512]{1,0:T(8,128)} %all-gather.5.cloned.1.call-done), kind=kOutput, calls=%fused_computation.5 | convolution fusion | flops 3221487616 | bytes 6291456 | tf_op jit(solution)/shard_map/dot_general | solution.py:36
  263.9 84.4 %reduce-scatter.5.cloned.1.call-done = f32[32,64]{1,0:T(8,128)} async-done(((f32[1024,64]{1,0:T(8,128)}), f32[32,64]{1,0:T(8,128)}) %reduce-scatter.5.cloned.1.call-update) | async-done | bytes 8208 | tf_op jit(solution)/shard_map/reduce_scatter | solution.py:51
  348.4 1.4 select_subtract_fusion
  349.8 104.3 %reduce-scatter.3.cloned.1.call-done = f32[32,512]{1,0:T(8,128)} async-done(((f32[1024,512]{1,0:T(8,128)}), f32[32,512]{1,0:T(8,128)}) %reduce-scatter.3.cloned.1.call-update) | async-done | bytes 65552 | tf_op jit(solution)/shard_map/reduce_scatter | solution.py:44
  454.0 1.5 sub.10
  (86 shorter events, 9.8 us)
Async XLA Ops:
  7.2 244.9 %copy-start = (f32[512,512]{1,0:T(8,128)S(1)}, f32[512,512]{1,0:T(8,128)}, u32[]{:S(2)}) copy-start(f32[512,512]{1,0:T(8,128)} %param.10) | copy-start | bytes 3145732
  7.2 116.0 %all-gather.3.cloned.1.call-start = ((), (), s32[]{:S(2)}) async-start(), calls=%async_computation.2 | async-start | bytes 6684672 | tf_op jit(solution)/shard_map/all_gather | solution.py:27
  37.1 220.5 %all-gather.5.cloned.1.call-start = ((), (), s32[]{:S(2)}) async-start(), calls=%async_computation.3 | async-start | bytes 2162688 | tf_op jit(solution)/shard_map/all_gather | solution.py:38
  37.8 310.5 %reduce-scatter.5.cloned.1.call-start = ((), (), s32[]{:S(2)}) async-start(), calls=%async_computation.5 | async-start | bytes 540672 | tf_op jit(solution)/shard_map/reduce_scatter | solution.py:51
  230.7 14.2 %copy-start.1 = (f32[8,128,128]{1,2,0:T(8,128)}, f32[8,128,128]{1,2,0:T(8,128)S(1)}, u32[]{:S(2)}) copy-start(f32[8,128,128]{1,2,0:T(8,128)S(1)} %custom-call.4) | copy-start | bytes 1572868
  247.7 1.5 copy-start.2
  251.8 202.2 %reduce-scatter.3.cloned.1.call-start = ((), (), s32[]{:S(2)}) async-start(), calls=%async_computation.4 | async-start | bytes 2162688 | tf_op jit(solution)/shard_map/reduce_scatter | solution.py:44
  257.5 90.8 %copy-start.4 = (f32[32,64]{1,0:T(8,128)S(1)}, f32[32,64]{1,0:T(8,128)}, u32[]{:S(2)}) copy-start(f32[32,64]{1,0:T(8,128)} %param.15) | copy-start | bytes 24580
  257.6 196.5 %copy-start.3 = (f32[32,512]{1,0:T(8,128)S(1)}, f32[32,512]{1,0:T(8,128)}, u32[]{:S(2)}) copy-start(f32[32,512]{1,0:T(8,128)} %param.14) | copy-start | bytes 196612
Sparse Core Ops, SparseCore 0:
  37.2 85.9 all-gather.2
  126.3 55.6 all-gather.4
  251.9 96.4 reduce-scatter.4
  352.6 101.3 reduce-scatter.2
